TPU v7x, 32 devices: a whole 2x2x4 slice. The times are simulated.
32 devices in a mesh: grp: 2 (over x), leaf: 8 (over z, y), sub: 2 (over core).
Axes of the slice: x: 2, y: 2, z: 4, core: 2. Of those that a mesh axis runs over, the one named last changes fastest.
Arguments:
- right_side: float32 [512, 2048], P(('grp', 'leaf', 'sub')), parts along dimension 0, may hold values from -24 to 24, as said below
- first_guess: float32 [512, 2048], P(('grp', 'leaf', 'sub')), parts along dimension 0, may hold values from -3 to 3
- couple: bfloat16 [512, 64, 384], P(('grp', 'leaf', 'sub')), parts along dimension 0, may hold values from -0.75 to 0.75
- send_lists: int32 [32, 2, 4], P(('grp', 'leaf', 'sub')), parts along dimension 0, may hold values from -1 to 15, as said below
- neighbours: int32 [512, 6], P(('grp', 'leaf', 'sub')), parts along dimension 0, may hold values from -1 to 23, as said below
Outputs:
- solution: float32 [512, 2048], P(('grp', 'leaf', 'sub')), parts along dimension 0
- residual: float32 [512, 2048], P(('grp', 'leaf', 'sub')), parts along dimension 0
There are 2 independent parts, one for each index of `grp`. A program takes and returns all parts, laid end to end along the dimension named above; each array names one. Nothing has to cross between parts.
Inputs may be any that keep to these rules, and one draw needn't show every extreme that they name: `right_side`: rows rise in scale along the element order. `send_lists`: for device d of a part and direction 0 (toward device d + 1) or 1 (toward device d - 1): distinct local element indices in the live slots, which come first, and -1 after them. The first device sends nothing in direction 1, the last nothing in direction 0; some device fills all 4 slots in direction 0 and the device after it all 4 in direction 1. `neighbours`: positions below 16 are the device's own elements, 16 + s the live slot s received from the previous device, 20 + s the live slot s received from the next device; -1 marks a face on the band's boundary.
All inputs are finite; a program needn't handle non-finite values.
Results may differ from a plain program's by a relative error of at most 0.034.
Values may be sent and summed in bfloat16 or wider, within the bound.
A program may use at most 64 MiB of HBM per device.

v0:
```python
import jax
import jax.numpy as jnp
from jax import lax
from jax.sharding import PartitionSpec as P

DOF = 64
FACES = 6
RHS = 32
SSTEP = 3
CYCLES = 4


def from_behind(value, axis, steps):
    count = lax.axis_size(axis)
    first, last = (max(0, -steps), min(count, count - steps))
    return lax.ppermute(value, axis, [(source, source + steps) for source in range(first, last)])


def couple_apply(vector_field, couple, send_lists, neighbours):
    local_count = vector_field.shape[0]
    slot_count = send_lists.shape[2]
    row_width = vector_field.shape[1]
    halves = vector_field.astype(jnp.bfloat16)
    own_lists = send_lists[0]
    chosen = jnp.take(halves, jnp.maximum(own_lists, 0).reshape(-1), axis=0).reshape(
        2, slot_count, row_width
    )
    chosen = jnp.where(own_lists[:, :, None] >= 0, chosen, jnp.zeros_like(chosen))
    forward = chosen[0]
    backward = chosen[1]
    before_blocks = from_behind(forward, ("leaf", "sub"), 1)
    after_blocks = from_behind(backward, ("leaf", "sub"), -1)
    zero_block = jnp.zeros((1, row_width), jnp.bfloat16)
    extended = jnp.concatenate([halves, before_blocks, after_blocks, zero_block], axis=0)
    positions = jnp.where(neighbours < 0, local_count + 2 * slot_count, neighbours).reshape(-1)
    gathered = jnp.take(extended, positions, axis=0).reshape(local_count, FACES * DOF, RHS)
    product = jnp.einsum("eik,ekr->eir", couple, gathered, preferred_element_type=jnp.float32)
    return product.reshape(local_count, DOF * RHS)


def to_columns(vector_field):
    return vector_field.reshape(-1, RHS)


def basis_sums(stacked):
    partial_sum = jnp.dot(
        stacked.T, stacked, precision=lax.Precision.HIGHEST, preferred_element_type=jnp.float32
    )
    total_sum = lax.psum(partial_sum, ("leaf", "sub"))
    return (total_sum[: SSTEP * RHS, : SSTEP * RHS], total_sum[: SSTEP * RHS, SSTEP * RHS :])


def shards(right_side, first_guess, couple, send_lists, neighbours):
    solution = first_guess
    residual = right_side - first_guess + couple_apply(first_guess, couple, send_lists, neighbours)
    for repeat in range(CYCLES):
        krylov_blocks = [residual]
        for degree in range(SSTEP):
            krylov_blocks.append(couple_apply(krylov_blocks[-1], couple, send_lists, neighbours))
        images = [
            krylov_blocks[order_index] - krylov_blocks[order_index + 1]
            for order_index in range(SSTEP)
        ]
        stacked = jnp.concatenate(
            [to_columns(image_block) for image_block in images] + [to_columns(residual)], axis=1
        )
        square_block, right_block = basis_sums(stacked)
        factor = jnp.linalg.cholesky(square_block)
        coeffs = jax.scipy.linalg.cho_solve((factor, True), right_block)
        krylov = jnp.concatenate(
            [to_columns(basis_block) for basis_block in krylov_blocks[:SSTEP]], axis=1
        )
        solution = solution + jnp.dot(
            krylov, coeffs, precision=lax.Precision.HIGHEST, preferred_element_type=jnp.float32
        ).reshape(solution.shape)
        residual = residual - jnp.dot(
            stacked[:, : SSTEP * RHS],
            coeffs,
            precision=lax.Precision.HIGHEST,
            preferred_element_type=jnp.float32,
        ).reshape(residual.shape)
    return (solution, residual)


def solution(mesh):
    placed = (
        P(("grp", "leaf", "sub"), None),
        P(("grp", "leaf", "sub"), None),
        P(("grp", "leaf", "sub"), None, None),
        P(("grp", "leaf", "sub"), None, None),
        P(("grp", "leaf", "sub"), None),
    )
    return jax.shard_map(
        shards,
        mesh=mesh,
        in_specs=placed,
        out_specs=(P(("grp", "leaf", "sub"), None), P(("grp", "leaf", "sub"), None)),
        check_vma=False,
    )
```

profile of v0, /device:TPU:0, one launch (start us, length us, event | category | flops | bytes accessed | tf_op | source)
XLA Modules:
  0.0 678.5 jit_solution(5330621828256337347)
XLA Ops:
  15.2 2.9 collective-permute-done.1
  22.3 4.4 collective-permute-start.2
  36.3 4.7 collective-permute-start.4
  50.1 4.8 collective-permute-start.6
  65.5 87.5 %all-reduce.5.cloned.1.call-done = f32[128,128]{0,1:T(8,128)} async-done(((f32[128,128]{0,1:T(8,128)}), f32[128,128]{0,1:T(8,128)}) %all-reduce.5.cloned.1.call-update) | async-done | bytes 65552 | tf_op jit(solution)/shard_map/psum | solution.py:49
  154.8 8.8 %cholesky.74 = f32[96,96]{1,0:T(8,128)S(1)} custom-call(f32[96,96]{1,0:T(8,128)S(1)} %fusion.103), custom_call_target="Cholesky" | custom-call | tf_op jit(solution)/shard_map/jit(cholesky)/cholesky | solution.py:68
  164.9 7.4 %custom-call.10 = f32[1,96,96]{1,2,0:T(8,128)S(1)} custom-call(f32[1,96,96]{2,1,0:T(8,128)S(1)} %fusion.80), custom_call_target="InvertDiagBlocksLowerTriangular" | custom-call | tf_op jit(solution)/shard_map/jit(_cho_solve)/triangular_solve | solution.py:69
  186.2 4.4 collective-permute-start.10
  192.3 3.1 collective-permute-done.11
  205.0 6.0 collective-permute-start.12
  223.6 86.4 %all-reduce.7.cloned.1.call-done = f32[128,128]{0,1:T(8,128)} async-done(((f32[128,128]{0,1:T(8,128)}), f32[128,128]{0,1:T(8,128)}) %all-reduce.7.cloned.1.call-update) | async-done | bytes 65552 | tf_op jit(solution)/shard_map/psum | solution.py:49
  311.7 8.8 %cholesky.85 = f32[96,96]{1,0:T(8,128)S(1)} custom-call(f32[96,96]{1,0:T(8,128)S(1)} %fusion.98), custom_call_target="Cholesky" | custom-call | tf_op jit(solution)/shard_map/jit(cholesky)/cholesky | solution.py:68
  321.8 7.4 %custom-call.11 = f32[1,96,96]{1,2,0:T(8,128)S(1)} custom-call(f32[1,96,96]{2,1,0:T(8,128)S(1)} %fusion.81), custom_call_target="InvertDiagBlocksLowerTriangular" | custom-call | tf_op jit(solution)/shard_map/jit(_cho_solve)/triangular_solve | solution.py:69
  347.3 4.4 collective-permute-start.16
  353.0 3.5 collective-permute-done.17
  366.2 6.0 collective-permute-start.18
  385.2 86.2 %all-reduce.9.cloned.1.call-done = f32[128,128]{0,1:T(8,128)} async-done(((f32[128,128]{0,1:T(8,128)}), f32[128,128]{0,1:T(8,128)}) %all-reduce.9.cloned.1.call-update) | async-done | bytes 65552 | tf_op jit(solution)/shard_map/psum | solution.py:49
  473.1 8.8 %cholesky.96 = f32[96,96]{1,0:T(8,128)S(1)} custom-call(f32[96,96]{1,0:T(8,128)S(1)} %fusion.93), custom_call_target="Cholesky" | custom-call | tf_op jit(solution)/shard_map/jit(cholesky)/cholesky | solution.py:68
  483.3 7.4 %custom-call.12 = f32[1,96,96]{1,2,0:T(8,128)S(1)} custom-call(f32[1,96,96]{2,1,0:T(8,128)S(1)} %fusion.82), custom_call_target="InvertDiagBlocksLowerTriangular" | custom-call | tf_op jit(solution)/shard_map/jit(_cho_solve)/triangular_solve | solution.py:69
  511.1 4.3 collective-permute-start.22
  532.4 5.3 collective-permute-start.24
  561.6 86.0 %all-reduce.11.cloned.1.call-done = f32[128,128]{0,1:T(8,128)} async-done(((f32[128,128]{0,1:T(8,128)}), f32[128,128]{0,1:T(8,128)}) %all-reduce.11.cloned.1.call-update) | async-done | bytes 65552 | tf_op jit(solution)/shard_map/psum | solution.py:49
  649.3 8.8 %cholesky.107 = f32[96,96]{1,0:T(8,128)S(1)} custom-call(f32[96,96]{1,0:T(8,128)S(1)} %fusion.88), custom_call_target="Cholesky" | custom-call | tf_op jit(solution)/shard_map/jit(cholesky)/cholesky | solution.py:68
  659.4 7.4 %custom-call.13 = f32[1,96,96]{1,2,0:T(8,128)S(1)} custom-call(f32[1,96,96]{2,1,0:T(8,128)S(1)} %fusion.83), custom_call_target="InvertDiagBlocksLowerTriangular" | custom-call | tf_op jit(solution)/shard_map/jit(_cho_solve)/triangular_solve | solution.py:69
  (484 shorter events, 197.7 us)
Async XLA Ops:
  7.2 145.9 %all-reduce.5.cloned.1.call-start = ((), (), s32[]{:S(2)}) async-start(), calls=%async_computation | async-start | bytes 131072 | tf_op jit(solution)/shard_map/psum | solution.py:49
  10.5 4.7 collective-permute-start
  12.9 5.2 collective-permute-start.1
  22.3 5.7 collective-permute-start.2
  36.3 6.0 collective-permute-start.4
  50.1 8.9 %collective-permute-start.6 = (bf16[4,2048]{1,0:T(4,128)(2,1)S(1)}, bf16[4,2048]{1,0:T(4,128)(2,1)S(1)}, u32[]{:S(2)}, u32[]{:S(2)}) collective-permute-start(bf16[4,2048]{1,0:T(4,128)(2,1)S(1)} %get-tuple-element.48), channel_id=1, source_target_pairs={{0,1},{1,2},{2,3},{3,4},{4,5},{5,6},{6,7},{7,8},{8,9},{9,10},{10,1... | collective-permute-start | bytes 49160 | tf_op jit(solution)/shard_map/ppermute | solution.py:16
  54.9 4.1 collective-permute-start.7
  65.5 244.5 %all-reduce.7.cloned.1.call-start = ((), (), s32[]{:S(2)}) async-start(), calls=%async_computation.1 | async-start | bytes 131072 | tf_op jit(solution)/shard_map/psum | solution.py:49
  186.2 6.1 collective-permute-start.10
  190.6 4.8 collective-permute-start.11
  205.0 11.2 %collective-permute-start.12 = (bf16[4,2048]{1,0:T(4,128)(2,1)}, bf16[4,2048]{1,0:T(4,128)(2,1)S(1)}, u32[]{:S(2)}, u32[]{:S(2)}) collective-permute-start(bf16[4,2048]{1,0:T(4,128)(2,1)} %get-tuple-element.42), channel_id=1, source_target_pairs={{0,1},{1,2},{2,3},{3,4},{4,5},{5,6},{6,7},{7,8},{8,9},{9,10},{10,1... | collective-permute-start | bytes 49160 | tf_op jit(solution)/shard_map/ppermute | solution.py:16
  211.0 5.2 collective-permute-start.13
  223.5 247.9 %all-reduce.9.cloned.1.call-start = ((), (), s32[]{:S(2)}) async-start(), calls=%async_computation.2 | async-start | bytes 131072 | tf_op jit(solution)/shard_map/psum | solution.py:49
  333.1 3.7 collective-permute-start.14
  347.3 5.7 collective-permute-start.16
  351.7 4.8 collective-permute-start.17
  366.2 11.5 %collective-permute-start.18 = (bf16[4,2048]{1,0:T(4,128)(2,1)}, bf16[4,2048]{1,0:T(4,128)(2,1)S(1)}, u32[]{:S(2)}, u32[]{:S(2)}) collective-permute-start(bf16[4,2048]{1,0:T(4,128)(2,1)} %get-tuple-element.36), channel_id=1, source_target_pairs={{0,1},{1,2},{2,3},{3,4},{4,5},{5,6},{6,7},{7,8},{8,9},{9,10},{10,1... | collective-permute-start | bytes 49160 | tf_op jit(solution)/shard_map/ppermute | solution.py:16
  372.2 5.5 collective-permute-start.19
  385.0 262.6 %all-reduce.11.cloned.1.call-start = ((), (), s32[]{:S(2)}) async-start(), calls=%async_computation.3 | async-start | bytes 131072 | tf_op jit(solution)/shard_map/psum | solution.py:49
  494.0 5.6 collective-permute-start.20
  511.1 11.6 %collective-permute-start.22 = (bf16[4,2048]{1,0:T(4,128)(2,1)S(1)}, bf16[4,2048]{1,0:T(4,128)(2,1)S(1)}, u32[]{:S(2)}, u32[]{:S(2)}) collective-permute-start(bf16[4,2048]{1,0:T(4,128)(2,1)S(1)} %get-tuple-element.32), channel_id=1, source_target_pairs={{0,1},{1,2},{2,3},{3,4},{4,5},{5,6},{6,7},{7,8},{8,9},{9,10},{10,1... | collective-permute-start | bytes 49160 | tf_op jit(solution)/shard_map/ppermute | solution.py:16
  515.4 7.2 %collective-permute-start.23 = (bf16[4,2048]{1,0:T(4,128)(2,1)S(1)}, bf16[4,2048]{1,0:T(4,128)(2,1)S(1)}, u32[]{:S(2)}, u32[]{:S(2)}) collective-permute-start(bf16[4,2048]{1,0:T(4,128)(2,1)S(1)} %get-tuple-element.33), channel_id=1, source_target_pairs={{1,0},{2,1},{3,2},{4,3},{5,4},{6,5},{7,6},{8,7},{9,8},{10,9},{11,1... | collective-permute-start | bytes 49160 | tf_op jit(solution)/shard_map/ppermute | solution.py:16
  532.4 15.2 %collective-permute-start.24 = (bf16[4,2048]{1,0:T(4,128)(2,1)}, bf16[4,2048]{1,0:T(4,128)(2,1)}, u32[]{:S(2)}, u32[]{:S(2)}) collective-permute-start(bf16[4,2048]{1,0:T(4,128)(2,1)} %get-tuple-element.30), channel_id=1, source_target_pairs={{0,1},{1,2},{2,3},{3,4},{4,5},{5,6},{6,7},{7,8},{8,9},{9,10},{10,1... | collective-permute-start | bytes 49160 | tf_op jit(solution)/shard_map/ppermute | solution.py:16
  537.7 9.9 %collective-permute-start.25 = (bf16[4,2048]{1,0:T(4,128)(2,1)}, bf16[4,2048]{1,0:T(4,128)(2,1)}, u32[]{:S(2)}, u32[]{:S(2)}) collective-permute-start(bf16[4,2048]{1,0:T(4,128)(2,1)} %get-tuple-element.31), channel_id=1, source_target_pairs={{1,0},{2,1},{3,2},{4,3},{5,4},{6,5},{7,6},{8,7},{9,8},{10,9},{11,1... | collective-permute-start | bytes 49160 | tf_op jit(solution)/shard_map/ppermute | solution.py:16
  (86 other events, 1717.7 us)
Sparse Core Ops, SparseCore 0:
  65.6 87.4 all-reduce.4
  223.6 86.2 all-reduce.6
  385.1 86.2 all-reduce.8
  557.8 89.6 all-reduce.10
where the time goes:
time: 688 us; the launch traced here: 679 us
  waiting for transfers between devices  363 us (53%)
  other arithmetic  104 us (15%)
  local copies, waits for them, and re-layouts  94.6 us (14%)
  starting transfers between devices  71.7 us (10%)
  matrix products  28.9 us (4%)
  between operations  16.5 us (2%)
    psum x4, waiting for transfers between devices, basis_sums(): total_sum = lax.psum(partial_sum, ('leaf', 'sub'))  346 us
    ppermute x26, starting transfers between devices, from_behind(): lax.ppermute(value, axis, [(source, source + steps) for source in range(f...  71.3 us
    another operation x12, other arithmetic, shards(): factor = jnp.linalg.cholesky(square_block)  37.9 us
    another operation x8, other arithmetic, shards(): coeffs = jax.scipy.linalg.cho_solve((factor, True), right_block)  32 us
    reshape x13, local copies, waits for them, and re-layouts, couple_apply(): jnp.take(extended, positions, axis=0).reshape(local_count, FACES * DOF, RHS)  27.4 us
    ppermute x26, waiting for transfers between devices, from_behind(): lax.ppermute(value, axis, [(source, source + steps) for source in range(f...  17 us
  transfers between devices with their start and end apart: 30, of which 11 were waited for; matrix products, arithmetic and copies ran while one was open for 5% of the time, Pallas kernels for 0%

commit v1 on v0

v1 whole, which is shorter than its diff:
```python
import functools

import jax
import jax.numpy as jnp
from jax import lax
from jax.experimental import pallas as pl
from jax.experimental.pallas import tpu as pltpu
from jax.sharding import PartitionSpec as P

DOF = 64
FACES = 6
RHS = 32
SSTEP = 3
CYCLES = 4
KEPT = SSTEP * RHS
WIDTH = KEPT + RHS
MESH = pl.DeviceIdType.MESH


def gauss_jordan(system):
    rows = lax.broadcasted_iota(jnp.int32, (KEPT, 1), 0)
    for k in range(KEPT):
        pivot_row = system[k : k + 1, :] / system[k : k + 1, k : k + 1]
        system = jnp.where(rows == k, pivot_row, system - system[:, k : k + 1] * pivot_row)
    return system[:, KEPT:]


def split(value):
    high = value.astype(jnp.bfloat16)
    return high, (value - high.astype(jnp.float32)).astype(jnp.bfloat16)


def kernel(
    leaves, subs, elems, slots,
    right_ref, guess_ref, couple_ref, lists_ref, near_ref,
    x_ref, r_ref,
    ext, basis, current, packed_out, packed_in, partial, arrived, total,
    halo_send, halo_recv, sum_send, sum_recv,
):
    count = leaves * subs
    share = WIDTH // count
    zero_at = elems + 2 * slots
    me = lax.axis_index("leaf") * subs + lax.axis_index("sub")

    def place(index):
        return {"leaf": lax.div(index, subs), "sub": lax.rem(index, subs)}

    def peer(step):
        return lax.rem(me + step, count)

    barrier = pltpu.get_barrier_semaphore()
    for step in range(1, count):
        pl.semaphore_signal(barrier, inc=1, device_id=place(peer(step)), device_id_type=MESH)
    pl.semaphore_wait(barrier, count - 1)

    for side in range(2):
        ext[side, elems:] = jnp.zeros((2 * slots + 1, DOF, RHS), jnp.bfloat16)

    def halo_copy(way, at, target):
        return pltpu.make_async_remote_copy(
            src_ref=packed_out.at[at, way],
            dst_ref=packed_in.at[at, way],
            send_sem=halo_send.at[at, way],
            recv_sem=halo_recv.at[at, way],
            device_id=place(target),
            device_id_type=MESH,
        )

    def exchange(side, at):
        for way in range(2):
            blocks = []
            for slot in range(slots):
                listed = lists_ref[0, way, slot]
                blocks.append(ext[side, jnp.where(listed < 0, zero_at, listed)])
            packed_out[at, way] = jnp.concatenate(blocks, axis=1)
        ahead = halo_copy(0, at, lax.rem(me + 1, count))
        back = halo_copy(1, at, lax.rem(me + count - 1, count))
        has_next = me < count - 1
        has_previous = me > 0

        @pl.when(has_next)
        def _():
            ahead.start()

        @pl.when(has_previous)
        def _():
            back.start()

        @pl.when(has_previous)
        def _():
            ahead.wait_recv()
            for slot in range(slots):
                ext[side, elems + slot] = packed_in[at, 0, :, slot * RHS : (slot + 1) * RHS]

        @pl.when(has_next)
        def _():
            back.wait_recv()
            for slot in range(slots):
                ext[side, elems + slots + slot] = packed_in[at, 1, :, slot * RHS : (slot + 1) * RHS]

        @pl.when(has_next)
        def _():
            ahead.wait_send()

        @pl.when(has_previous)
        def _():
            back.wait_send()

    def applied(side, element):
        blocks = []
        for face in range(FACES):
            near = near_ref[element, face]
            blocks.append(ext[side, jnp.where(near < 0, zero_at, near)])
        gathered = jnp.concatenate(blocks, axis=0)
        return jnp.dot(couple_ref[element], gathered, preferred_element_type=jnp.float32)

    def rows_of(element):
        return slice(element * DOF, (element + 1) * DOF)

    def keep(rows, order, value):
        high, low = split(value)
        basis[rows, order * RHS : (order + 1) * RHS] = high
        basis[rows, WIDTH + order * RHS : WIDTH + (order + 1) * RHS] = low
        return high

    for element in range(elems):
        guess = guess_ref[rows_of(element), :]
        x_ref[rows_of(element), :] = guess
        ext[1, element] = guess.astype(jnp.bfloat16)
    exchange(1, SSTEP)
    for element in range(elems):
        rows = rows_of(element)
        first = right_ref[rows, :] - guess_ref[rows, :] + applied(1, element)
        r_ref[rows, :] = first
        ext[0, element] = keep(rows, SSTEP, first)

    def sum_copy(source, target, step, phase):
        return pltpu.make_async_remote_copy(
            src_ref=source,
            dst_ref=target,
            send_sem=sum_send.at[phase],
            recv_sem=sum_recv.at[phase],
            device_id=place(peer(step)),
            device_id_type=MESH,
        )

    def cycle(repeat, carry):
        for order in range(SSTEP):
            side = order % 2
            exchange(side, order)
            for element in range(elems):
                rows = rows_of(element)
                image = applied(side, element)
                before = r_ref[rows, :] if order == 0 else current[rows, :]
                keep(rows, order, before - image)
                if order < SSTEP - 1:
                    current[rows, :] = image
                    ext[1 - side, element] = image.astype(jnp.bfloat16)

        products = lax.dot_general(
            basis[:, :WIDTH], basis[...], (((0,), (0,)), ((), ())),
            preferred_element_type=jnp.float32,
        )
        cross = products[:, WIDTH:]
        gram = products[:, :WIDTH] + cross + cross.T
        for shard in range(count):
            partial[shard] = gram[shard * share : (shard + 1) * share, :]
        for step in range(1, count):
            sum_copy(partial.at[peer(step)], arrived.at[step], step, 0).start()
        rest = pl.ds(1, count - 1)
        whole = sum_copy(partial.at[rest], arrived.at[rest], 1, 0)
        whole.wait_recv()
        reduced = partial[me]
        for step in range(1, count):
            reduced = reduced + arrived[step]
        total[me] = reduced
        for step in range(1, count):
            sum_copy(total.at[me], total.at[me], step, 1).start()
        whole.wait_send()
        both = sum_copy(total.at[rest], total.at[rest], 1, 1)
        both.wait_recv()
        both.wait_send()
        system = jnp.concatenate(
            [total[shard] for shard in range(count)], axis=0
        )[:KEPT]
        coeffs = gauss_jordan(system)

        c0, c1, c2 = coeffs[:RHS], coeffs[RHS : 2 * RHS], coeffs[2 * RHS :]
        nothing = jnp.zeros((RHS, RHS), jnp.float32)
        late = c1 + c2
        down = jnp.concatenate([c0, c1, c2, nothing], axis=0)
        up = jnp.concatenate([-late, -c2, nothing, c0 + late], axis=0)
        high, low = split(jnp.concatenate([down, up], axis=1))
        factor = jnp.concatenate(
            [
                jnp.concatenate([high, low], axis=1),
                jnp.concatenate([high, jnp.zeros_like(low)], axis=1),
            ],
            axis=0,
        )
        for element in range(elems):
            rows = rows_of(element)
            change = jnp.dot(basis[rows, :], factor, preferred_element_type=jnp.float32)
            change = change[:, : 2 * RHS] + change[:, 2 * RHS :]
            x_ref[rows, :] = x_ref[rows, :] + change[:, RHS:]
            later = r_ref[rows, :] - change[:, :RHS]
            r_ref[rows, :] = later
            ext[0, element] = keep(rows, SSTEP, later)
        return carry

    lax.fori_loop(0, CYCLES, cycle, 0)


def shards(leaves, subs, right_side, first_guess, couple, send_lists, neighbours):
    elems, _, _ = couple.shape
    slots = send_lists.shape[2]
    count = leaves * subs
    share = WIDTH // count
    rows = elems * DOF
    vmem = pl.BlockSpec(memory_space=pltpu.VMEM)
    smem = pl.BlockSpec(memory_space=pltpu.SMEM)
    field = jax.ShapeDtypeStruct((rows, RHS), jnp.float32)
    x, r = pl.pallas_call(
        functools.partial(kernel, leaves, subs, elems, slots),
        out_shape=(field, field),
        in_specs=[vmem, vmem, vmem, smem, smem],
        out_specs=(vmem, vmem),
        scratch_shapes=[
            pltpu.VMEM((2, elems + 2 * slots + 1, DOF, RHS), jnp.bfloat16),
            pltpu.VMEM((rows, 2 * WIDTH), jnp.bfloat16),
            pltpu.VMEM((rows, RHS), jnp.float32),
            pltpu.VMEM((SSTEP + 1, 2, DOF, slots * RHS), jnp.bfloat16),
            pltpu.VMEM((SSTEP + 1, 2, DOF, slots * RHS), jnp.bfloat16),
            pltpu.VMEM((count, share, WIDTH), jnp.float32),
            pltpu.VMEM((count, share, WIDTH), jnp.float32),
            pltpu.VMEM((count, share, WIDTH), jnp.float32),
            pltpu.SemaphoreType.DMA((SSTEP + 1, 2)),
            pltpu.SemaphoreType.DMA((SSTEP + 1, 2)),
            pltpu.SemaphoreType.DMA((2,)),
            pltpu.SemaphoreType.DMA((2,)),
        ],
        compiler_params=pltpu.CompilerParams(
            collective_id=0, has_side_effects=True, vmem_limit_bytes=40 * 1024 * 1024
        ),
    )(
        right_side.reshape(rows, RHS), first_guess.reshape(rows, RHS),
        couple, send_lists, neighbours,
    )
    return x.reshape(right_side.shape), r.reshape(right_side.shape)


def solution(mesh):
    lead = ("grp", "leaf", "sub")
    flat, deep = P(lead, None), P(lead, None, None)
    return jax.shard_map(
        functools.partial(shards, mesh.shape["leaf"], mesh.shape["sub"]),
        mesh=mesh,
        in_specs=(flat, flat, deep, deep, flat),
        out_specs=(flat, flat),
        check_vma=False,
    )
```

time: 688 us -> 145 us (0.21); the launches traced: 679 us -> 145 us
  waiting for transfers between devices: 363 us -> 0 us
  Pallas kernels: 0 us -> 139 us
  other arithmetic: 104 us -> 0 us
  local copies, waits for them, and re-layouts: 94.6 us -> 4.77 us
  starting transfers between devices: 71.7 us -> 0 us
  matrix products: 28.9 us -> 0 us
  between operations: 16.5 us -> 0.69 us
    psum x4 -> x0, waiting for transfers between devices: 346 us -> none  [basis_sums(): total_sum = lax.psum(partial_sum, ('leaf', 'sub'))]
    pallas_call x0 -> x1, Pallas kernels: none -> 139 us  [shards(): pl.pallas_call(functools.partial(kernel, leaves, subs, elems, slots), out...]
    ppermute x26 -> x0, starting transfers between devices: 71.3 us -> none  [from_behind(): lax.ppermute(value, axis, [(source, source + steps) for source in range(f...]
    another operation x20 -> x0, other arithmetic: 69.9 us -> none  [the longest x12 37.9 us: shards(): factor = jnp.linalg.cholesky(square_block)]
    reshape x60 -> x4, local copies, waits for them, and re-layouts: 43.6 us -> 3.93 us  [the longest x2 1.78 us: shards(): return (x.reshape(right_side.shape), r.reshape(right_side.shape))]
    dot_general x25 -> x0, matrix products: 24.7 us -> none  [the longest x13 11.1 us: couple_apply(): jnp.einsum('eik,ekr->eir', couple, gathered, preferred_element_type=jnp.f...]
    gather x26 -> x0, local copies, waits for them, and re-layouts: 20.8 us -> none  [the longest x13 12.1 us: couple_apply(): jnp.take(extended, positions, axis=0).reshape(local_count, FACES * DOF, RHS)]
    select_n x42 -> x0, other arithmetic: 17.6 us -> none  [the longest x14 9.56 us: couple_apply(): jnp.take(extended, positions, axis=0).reshape(local_count, FACES * DOF, RHS)]
  transfers between devices with their start and end apart: 30 -> 0, of which waited for: 11 -> 0; matrix products, arithmetic and copies ran while one was open for 5% -> 0% of each run, Pallas kernels for 0% -> 0%
where the time goes in v1:
time: 145 us
  Pallas kernels  139 us (96%)
  local copies, waits for them, and re-layouts  4.77 us (3%)
    pallas_call x1, Pallas kernels, shards(): pl.pallas_call(functools.partial(kernel, leaves, subs, elems, slots), out...  139 us

profile of v1, /device:TPU:0, one launch (start us, length us, event | category | flops | bytes accessed | tf_op | source)
XLA Modules:
  0.0 144.8 jit_solution(893331397653420819)
XLA Ops:
  0.6 0.0 copy-start
  0.6 0.8 copy.8.near_ref
  1.5 1.1 reshape.16.right_ref
  2.6 0.0 copy-start.1
  2.6 1.1 reshape.17.guess_ref
  3.7 0.0 copy-done
  3.7 0.0 copy-done.1
  3.7 139.3 %shard_map.68 = (f32[1024,32]{1,0:T(8,128)S(1)}, f32[1024,32]{1,0:T(8,128)S(1)}) custom-call(f32[1024,32]{1,0:T(8,128)S(1)} %reshape.16.right_ref, f32[1024,32]{1,0:T(8,128)S(1)} %reshape.17.guess_ref, bf16[16,64,384]{2,1,0:T(8,128)(2,1)S(1)} %copy-done, s32[1,2,4]{2,1,0:T(2,128)S(1)} %copy-done.1, s32[16,6]{1,0:T(8,128)S(1)} %copy.8.near_ref), custom_call_target="tpu_custom_call" | custom-call | tf_op jit(solution)/shard_map/pallas_call | solution.py:223
  143.0 0.9 reshape.18
  143.9 0.9 reshape.19
Async XLA Ops:
  0.6 3.0 %copy-start = (bf16[16,64,384]{2,1,0:T(8,128)(2,1)S(1)}, bf16[16,64,384]{2,1,0:T(8,128)(2,1)}, u32[]{:S(2)}) copy-start(bf16[16,64,384]{2,1,0:T(8,128)(2,1)} %couple_ref.1) | copy-start | bytes 2359300
  2.6 1.1 copy-start.1

commit v2 on v1

--- a/solution.py
+++ b/solution.py
@@ -18,11 +18,37 @@
 
 
 def gauss_jordan(system):
-    rows = lax.broadcasted_iota(jnp.int32, (KEPT, 1), 0)
-    for k in range(KEPT):
-        pivot_row = system[k : k + 1, :] / system[k : k + 1, k : k + 1]
-        system = jnp.where(rows == k, pivot_row, system - system[:, k : k + 1] * pivot_row)
-    return system[:, KEPT:]
+    tile = 8
+    tiles = [system[first : first + tile] for first in range(0, KEPT, tile)]
+    rows = lax.broadcasted_iota(jnp.int32, (tile, WIDTH), 0)
+
+    def columns(value, at):
+        first = at * tile
+        return [
+            jnp.broadcast_to(value[:, first + k : first + k + 1], (tile, WIDTH))
+            for k in range(tile)
+        ]
+
+    for at in range(len(tiles)):
+        block, factors = tiles[at], columns(tiles[at], at)
+        outside = [columns(value, at) if i != at else None for i, value in enumerate(tiles)]
+        for k in range(tile):
+            inverse = 1.0 / factors[k][k : k + 1, :]
+
+            def eliminated(value):
+                pivot_row = value[k : k + 1, :] * inverse
+                return jnp.where(rows == k, pivot_row, value - factors[k] * pivot_row)
+
+            block = eliminated(block)
+            factors = factors[: k + 1] + [eliminated(value) for value in factors[k + 1 :]]
+        tiles[at] = block
+        for i in range(len(tiles)):
+            if i != at:
+                value = tiles[i]
+                for k in range(tile):
+                    value = value - outside[i][k] * block[k : k + 1, :]
+                tiles[i] = value
+    return jnp.concatenate(tiles, axis=0)[:, KEPT:]
 
 
 def split(value):

time: 145 us -> 121 us (0.83)
  Pallas kernels: 139 us -> 115 us
    pallas_call x1, Pallas kernels: 139 us -> 115 us  [shards(): pl.pallas_call(functools.partial(kernel, leaves, subs, elems, slots), out...]
where the time goes in v2:
time: 121 us
  Pallas kernels  115 us (95%)
  local copies, waits for them, and re-layouts  4.77 us (4%)
    pallas_call x1, Pallas kernels, shards(): pl.pallas_call(functools.partial(kernel, leaves, subs, elems, slots), out...  115 us

profile of v2, /device:TPU:0, one launch (start us, length us, event | category | flops | bytes accessed | tf_op | source)
XLA Modules:
  0.0 120.9 jit_solution(9190513148976655795)
XLA Ops:
  0.6 0.0 copy-start
  0.6 0.8 copy.8.near_ref
  1.5 1.1 reshape.16.right_ref
  2.6 0.0 copy-start.1
  2.6 1.1 reshape.17.guess_ref
  3.7 0.0 copy-done
  3.7 0.0 copy-done.1
  3.7 115.5 %shard_map.68 = (f32[1024,32]{1,0:T(8,128)S(1)}, f32[1024,32]{1,0:T(8,128)S(1)}) custom-call(f32[1024,32]{1,0:T(8,128)S(1)} %reshape.16.right_ref, f32[1024,32]{1,0:T(8,128)S(1)} %reshape.17.guess_ref, bf16[16,64,384]{2,1,0:T(8,128)(2,1)S(1)} %copy-done, s32[1,2,4]{2,1,0:T(2,128)S(1)} %copy-done.1, s32[16,6]{1,0:T(8,128)S(1)} %copy.8.near_ref), custom_call_target="tpu_custom_call" | custom-call | tf_op jit(solution)/shard_map/pallas_call | solution.py:249
  119.1 0.9 reshape.18
  120.0 0.9 reshape.19
Async XLA Ops:
  0.6 3.0 %copy-start = (bf16[16,64,384]{2,1,0:T(8,128)(2,1)S(1)}, bf16[16,64,384]{2,1,0:T(8,128)(2,1)}, u32[]{:S(2)}) copy-start(bf16[16,64,384]{2,1,0:T(8,128)(2,1)} %couple_ref.1) | copy-start | bytes 2359300
  2.6 1.1 copy-start.1

commit v3 on v2

--- a/solution.py
+++ b/solution.py
@@ -60,23 +60,39 @@
     leaves, subs, elems, slots,
     right_ref, guess_ref, couple_ref, lists_ref, near_ref,
     x_ref, r_ref,
-    ext, basis, current, packed_out, packed_in, partial, arrived, total,
+    ext, basis, current, power_one, power_two, packed_out, packed_in, partial, arrived, total,
     halo_send, halo_recv, sum_send, sum_recv,
 ):
     count = leaves * subs
     share = WIDTH // count
     zero_at = elems + 2 * slots
-    me = lax.axis_index("leaf") * subs + lax.axis_index("sub")
-
-    def place(index):
-        return {"leaf": lax.div(index, subs), "sub": lax.rem(index, subs)}
+    grp, leaf, sub = (lax.axis_index(name) for name in ("grp", "leaf", "sub"))
+    me = leaf * subs + sub
+    steps = [(far, near) for far in range(leaves) for near in range(subs)][1:]
+
+    def turned(value, step, size):
+        moved = value + step
+        return jnp.where(moved >= size, moved - size, moved)
+
+    def place(step):
+        return (grp, turned(leaf, step[0], leaves), turned(sub, step[1], subs))
 
     def peer(step):
-        return lax.rem(me + step, count)
+        return turned(leaf, step[0], leaves) * subs + turned(sub, step[1], subs)
+
+    last_sub, first_sub = sub == subs - 1, sub == 0
+    following = (
+        grp, turned(leaf, jnp.where(last_sub, 1, 0), leaves), jnp.where(last_sub, 0, sub + 1)
+    )
+    preceding = (
+        grp,
+        turned(leaf, jnp.where(first_sub, leaves - 1, 0), leaves),
+        jnp.where(first_sub, subs - 1, sub - 1),
+    )
 
     barrier = pltpu.get_barrier_semaphore()
-    for step in range(1, count):
-        pl.semaphore_signal(barrier, inc=1, device_id=place(peer(step)), device_id_type=MESH)
+    for step in steps:
+        pl.semaphore_signal(barrier, inc=1, device_id=place(step), device_id_type=MESH)
     pl.semaphore_wait(barrier, count - 1)
 
     for side in range(2):
@@ -88,7 +104,7 @@
             dst_ref=packed_in.at[at, way],
             send_sem=halo_send.at[at, way],
             recv_sem=halo_recv.at[at, way],
-            device_id=place(target),
+            device_id=target,
             device_id_type=MESH,
         )
 
@@ -99,8 +115,8 @@
                 listed = lists_ref[0, way, slot]
                 blocks.append(ext[side, jnp.where(listed < 0, zero_at, listed)])
             packed_out[at, way] = jnp.concatenate(blocks, axis=1)
-        ahead = halo_copy(0, at, lax.rem(me + 1, count))
-        back = halo_copy(1, at, lax.rem(me + count - 1, count))
+        ahead = halo_copy(0, at, following)
+        back = halo_copy(1, at, preceding)
         has_next = me < count - 1
         has_previous = me > 0
 
@@ -145,9 +161,24 @@
 
     def keep(rows, order, value):
         high, low = split(value)
-        basis[rows, order * RHS : (order + 1) * RHS] = high
-        basis[rows, WIDTH + order * RHS : WIDTH + (order + 1) * RHS] = low
+        if order <= SSTEP:
+            at, below = order * RHS, WIDTH + order * RHS
+        else:
+            at = 2 * WIDTH + (order - SSTEP - 1) * RHS
+            below = at + 2 * RHS
+        basis[rows, at : at + RHS] = high
+        basis[rows, below : below + RHS] = low
         return high
+
+    def advance(side, at, order, store):
+        exchange(side, at)
+        for element in range(elems):
+            rows = rows_of(element)
+            image = applied(side, element)
+            keep(rows, order, current[rows, :] - image)
+            if store:
+                current[rows, :] = image
+                ext[1 - side, element] = image.astype(jnp.bfloat16)
 
     for element in range(elems):
         guess = guess_ref[rows_of(element), :]
@@ -160,50 +191,57 @@
         r_ref[rows, :] = first
         ext[0, element] = keep(rows, SSTEP, first)
 
+    exchange(0, 0)
+    for element in range(elems):
+        rows = rows_of(element)
+        image = applied(0, element)
+        keep(rows, 0, r_ref[rows, :] - image)
+        power_one[rows, :] = image
+        ext[1, element] = image.astype(jnp.bfloat16)
+    exchange(1, 1)
+    for element in range(elems):
+        rows = rows_of(element)
+        image = applied(1, element)
+        keep(rows, 1, power_one[rows, :] - image)
+        power_two[rows, :] = image
+        current[rows, :] = image
+        ext[0, element] = image.astype(jnp.bfloat16)
+
     def sum_copy(source, target, step, phase):
         return pltpu.make_async_remote_copy(
             src_ref=source,
             dst_ref=target,
             send_sem=sum_send.at[phase],
             recv_sem=sum_recv.at[phase],
-            device_id=place(peer(step)),
+            device_id=place(step),
             device_id_type=MESH,
         )
 
     def cycle(repeat, carry):
-        for order in range(SSTEP):
-            side = order % 2
-            exchange(side, order)
-            for element in range(elems):
-                rows = rows_of(element)
-                image = applied(side, element)
-                before = r_ref[rows, :] if order == 0 else current[rows, :]
-                keep(rows, order, before - image)
-                if order < SSTEP - 1:
-                    current[rows, :] = image
-                    ext[1 - side, element] = image.astype(jnp.bfloat16)
-
+        advance(0, 0, 2, True)
         products = lax.dot_general(
-            basis[:, :WIDTH], basis[...], (((0,), (0,)), ((), ())),
+            basis[:, :WIDTH], basis[:, : 2 * WIDTH], (((0,), (0,)), ((), ())),
             preferred_element_type=jnp.float32,
         )
         cross = products[:, WIDTH:]
         gram = products[:, :WIDTH] + cross + cross.T
         for shard in range(count):
             partial[shard] = gram[shard * share : (shard + 1) * share, :]
-        for step in range(1, count):
-            sum_copy(partial.at[peer(step)], arrived.at[step], step, 0).start()
+        for slot, step in enumerate(steps):
+            sum_copy(partial.at[peer(step)], arrived.at[slot + 1], step, 0).start()
         rest = pl.ds(1, count - 1)
-        whole = sum_copy(partial.at[rest], arrived.at[rest], 1, 0)
+        whole = sum_copy(partial.at[rest], arrived.at[rest], steps[0], 0)
+        advance(1, 1, 4, True)
         whole.wait_recv()
         reduced = partial[me]
         for step in range(1, count):
             reduced = reduced + arrived[step]
         total[me] = reduced
-        for step in range(1, count):
+        for step in steps:
             sum_copy(total.at[me], total.at[me], step, 1).start()
         whole.wait_send()
-        both = sum_copy(total.at[rest], total.at[rest], 1, 1)
+        both = sum_copy(total.at[rest], total.at[rest], steps[0], 1)
+        advance(0, 2, 5, False)
         both.wait_recv()
         both.wait_send()
         system = jnp.concatenate(
@@ -214,24 +252,38 @@
         c0, c1, c2 = coeffs[:RHS], coeffs[RHS : 2 * RHS], coeffs[2 * RHS :]
         nothing = jnp.zeros((RHS, RHS), jnp.float32)
         late = c1 + c2
-        down = jnp.concatenate([c0, c1, c2, nothing], axis=0)
-        up = jnp.concatenate([-late, -c2, nothing, c0 + late], axis=0)
-        high, low = split(jnp.concatenate([down, up], axis=1))
         factor = jnp.concatenate(
             [
-                jnp.concatenate([high, low], axis=1),
-                jnp.concatenate([high, jnp.zeros_like(low)], axis=1),
+                jnp.concatenate([c0, c1, c2, nothing, nothing, nothing], axis=0),
+                jnp.concatenate([-late, -c2, nothing, c0 + late, nothing, nothing], axis=0),
+                jnp.concatenate([nothing, c0, c1, nothing, c2, nothing], axis=0),
+                jnp.concatenate([nothing, nothing, c0, nothing, c1, c2], axis=0),
             ],
+            axis=1,
+        )
+        high, low = split(factor)
+        left = jnp.concatenate([high[:WIDTH], high[:WIDTH], high[WIDTH:], high[WIDTH:]], axis=0)
+        right = jnp.concatenate(
+            [low[:WIDTH], jnp.zeros_like(low[:WIDTH]), low[WIDTH:], jnp.zeros_like(low[WIDTH:])],
             axis=0,
         )
+        factor = jnp.concatenate([left, right], axis=1)
         for element in range(elems):
             rows = rows_of(element)
             change = jnp.dot(basis[rows, :], factor, preferred_element_type=jnp.float32)
-            change = change[:, : 2 * RHS] + change[:, 2 * RHS :]
-            x_ref[rows, :] = x_ref[rows, :] + change[:, RHS:]
+            change = change[:, :WIDTH] + change[:, WIDTH:]
+            x_ref[rows, :] = x_ref[rows, :] + change[:, RHS : 2 * RHS]
             later = r_ref[rows, :] - change[:, :RHS]
+            one = power_one[rows, :] - change[:, 2 * RHS : 3 * RHS]
+            two = power_two[rows, :] - change[:, 3 * RHS :]
             r_ref[rows, :] = later
-            ext[0, element] = keep(rows, SSTEP, later)
+            power_one[rows, :] = one
+            power_two[rows, :] = two
+            current[rows, :] = two
+            ext[0, element] = two.astype(jnp.bfloat16)
+            keep(rows, SSTEP, later)
+            keep(rows, 0, later - one)
+            keep(rows, 1, one - two)
         return carry
 
     lax.fori_loop(0, CYCLES, cycle, 0)
@@ -253,7 +305,9 @@
         out_specs=(vmem, vmem),
         scratch_shapes=[
             pltpu.VMEM((2, elems + 2 * slots + 1, DOF, RHS), jnp.bfloat16),
-            pltpu.VMEM((rows, 2 * WIDTH), jnp.bfloat16),
+            pltpu.VMEM((rows, 2 * WIDTH + 4 * RHS), jnp.bfloat16),
+            pltpu.VMEM((rows, RHS), jnp.float32),
+            pltpu.VMEM((rows, RHS), jnp.float32),
             pltpu.VMEM((rows, RHS), jnp.float32),
             pltpu.VMEM((SSTEP + 1, 2, DOF, slots * RHS), jnp.bfloat16),
             pltpu.VMEM((SSTEP + 1, 2, DOF, slots * RHS), jnp.bfloat16),

time: 121 us -> 107 us (0.88)
  Pallas kernels: 115 us -> 102 us
    pallas_call x1, Pallas kernels: 115 us -> 102 us  [shards(): pl.pallas_call(functools.partial(kernel, leaves, subs, elems, slots), out...]
where the time goes in v3:
time: 107 us
  Pallas kernels  102 us (95%)
  local copies, waits for them, and re-layouts  4.77 us (4%)
    pallas_call x1, Pallas kernels, shards(): pl.pallas_call(functools.partial(kernel, leaves, subs, elems, slots), out...  102 us

profile of v3, /device:TPU:0, one launch (start us, length us, event | category | flops | bytes accessed | tf_op | source)
XLA Modules:
  0.0 107.0 jit_solution(11533952940234797011)
XLA Ops:
  0.6 0.0 copy-start
  0.6 0.8 copy.8.near_ref
  1.5 1.1 %reshape.16.right_ref = f32[1024,32]{1,0:T(8,128)S(1)} reshape(f32[16,2048]{1,0:T(8,128)} %param.5) | data formatting | bytes 262144 | tf_op jit(solution)/shard_map/reshape | solution.py:326
  2.6 0.0 copy-start.1
  2.6 1.1 %reshape.17.guess_ref = f32[1024,32]{1,0:T(8,128)S(1)} reshape(f32[16,2048]{1,0:T(8,128)} %param.6) | data formatting | bytes 262144 | tf_op jit(solution)/shard_map/reshape | solution.py:326
  3.7 0.0 copy-done
  3.7 0.0 copy-done.1
  3.7 101.5 %shard_map.68 = (f32[1024,32]{1,0:T(8,128)S(1)}, f32[1024,32]{1,0:T(8,128)S(1)}) custom-call(f32[1024,32]{1,0:T(8,128)S(1)} %reshape.16.right_ref, f32[1024,32]{1,0:T(8,128)S(1)} %reshape.17.guess_ref, bf16[16,64,384]{2,1,0:T(8,128)(2,1)S(1)} %copy-done, s32[1,2,4]{2,1,0:T(2,128)S(1)} %copy-done.1, s32[16,6]{1,0:T(8,128)S(1)} %copy.8.near_ref), custom_call_target="tpu_custom_call" | custom-call | tf_op jit(solution)/shard_map/pallas_call | solution.py:301
  105.2 0.9 reshape.18
  106.1 0.9 reshape.19
Async XLA Ops:
  0.6 3.0 %copy-start = (bf16[16,64,384]{2,1,0:T(8,128)(2,1)S(1)}, bf16[16,64,384]{2,1,0:T(8,128)(2,1)}, u32[]{:S(2)}) copy-start(bf16[16,64,384]{2,1,0:T(8,128)(2,1)} %couple_ref.1) | copy-start | bytes 2359300
  2.6 1.1 %copy-start.1 = (s32[1,2,4]{2,1,0:T(2,128)S(1)}, s32[1,2,4]{2,1,0:T(2,128)}, u32[]{:S(2)}) copy-start(s32[1,2,4]{2,1,0:T(2,128)} %lists_ref.1) | copy-start | bytes 100

commit v4 on v3

--- a/solution.py
+++ b/solution.py
@@ -108,25 +108,32 @@
             device_id_type=MESH,
         )
 
-    def exchange(side, at):
-        for way in range(2):
+    def exchange(side, at, meanwhile=None):
+        def pack(way):
             blocks = []
             for slot in range(slots):
                 listed = lists_ref[0, way, slot]
                 blocks.append(ext[side, jnp.where(listed < 0, zero_at, listed)])
             packed_out[at, way] = jnp.concatenate(blocks, axis=1)
+
         ahead = halo_copy(0, at, following)
         back = halo_copy(1, at, preceding)
         has_next = me < count - 1
         has_previous = me > 0
+        pack(0)
 
         @pl.when(has_next)
         def _():
             ahead.start()
 
+        pack(1)
+
         @pl.when(has_previous)
         def _():
             back.start()
+
+        if meanwhile is not None:
+            meanwhile()
 
         @pl.when(has_previous)
         def _():
@@ -170,8 +177,8 @@
         basis[rows, below : below + RHS] = low
         return high
 
-    def advance(side, at, order, store):
-        exchange(side, at)
+    def advance(side, at, order, store, meanwhile=None):
+        exchange(side, at, meanwhile)
         for element in range(elems):
             rows = rows_of(element)
             image = applied(side, element)
@@ -189,20 +196,18 @@
         rows = rows_of(element)
         first = right_ref[rows, :] - guess_ref[rows, :] + applied(1, element)
         r_ref[rows, :] = first
-        ext[0, element] = keep(rows, SSTEP, first)
+        ext[0, element] = first.astype(jnp.bfloat16)
 
     exchange(0, 0)
     for element in range(elems):
         rows = rows_of(element)
         image = applied(0, element)
-        keep(rows, 0, r_ref[rows, :] - image)
         power_one[rows, :] = image
         ext[1, element] = image.astype(jnp.bfloat16)
     exchange(1, 1)
     for element in range(elems):
         rows = rows_of(element)
         image = applied(1, element)
-        keep(rows, 1, power_one[rows, :] - image)
         power_two[rows, :] = image
         current[rows, :] = image
         ext[0, element] = image.astype(jnp.bfloat16)
@@ -217,8 +222,16 @@
             device_id_type=MESH,
         )
 
+    def refresh():
+        for element in range(elems):
+            rows = rows_of(element)
+            zero, one, two = r_ref[rows, :], power_one[rows, :], power_two[rows, :]
+            keep(rows, SSTEP, zero)
+            keep(rows, 0, zero - one)
+            keep(rows, 1, one - two)
+
     def cycle(repeat, carry):
-        advance(0, 0, 2, True)
+        advance(0, 0, 2, True, refresh)
         products = lax.dot_general(
             basis[:, :WIDTH], basis[:, : 2 * WIDTH], (((0,), (0,)), ((), ())),
             preferred_element_type=jnp.float32,
@@ -281,9 +294,6 @@
             power_two[rows, :] = two
             current[rows, :] = two
             ext[0, element] = two.astype(jnp.bfloat16)
-            keep(rows, SSTEP, later)
-            keep(rows, 0, later - one)
-            keep(rows, 1, one - two)
         return carry
 
     lax.fori_loop(0, CYCLES, cycle, 0)

time: 107 us -> 104 us (0.972)
  Pallas kernels: 102 us -> 98.5 us
    pallas_call x1, Pallas kernels: 102 us -> 98.5 us  [shards(): pl.pallas_call(functools.partial(kernel, leaves, subs, elems, slots), out...]
where the time goes in v4:
time: 104 us
  Pallas kernels  98.5 us (95%)
  local copies, waits for them, and re-layouts  4.77 us (5%)
    pallas_call x1, Pallas kernels, shards(): pl.pallas_call(functools.partial(kernel, leaves, subs, elems, slots), out...  98.5 us

profile of v4, /device:TPU:0, one launch (start us, length us, event | category | flops | bytes accessed | tf_op | source)
XLA Modules:
  0.0 104.0 jit_solution(10545897558632296212)
XLA Ops:
  0.6 0.0 copy-start
  0.6 0.8 copy.8.near_ref
  1.5 1.1 %reshape.16.right_ref = f32[1024,32]{1,0:T(8,128)S(1)} reshape(f32[16,2048]{1,0:T(8,128)} %param.5) | data formatting | bytes 262144 | tf_op jit(solution)/shard_map/reshape | solution.py:336
  2.6 0.0 copy-start.1
  2.6 1.1 %reshape.17.guess_ref = f32[1024,32]{1,0:T(8,128)S(1)} reshape(f32[16,2048]{1,0:T(8,128)} %param.6) | data formatting | bytes 262144 | tf_op jit(solution)/shard_map/reshape | solution.py:336
  3.7 0.0 copy-done
  3.7 0.0 copy-done.1
  3.7 98.5 %shard_map.68 = (f32[1024,32]{1,0:T(8,128)S(1)}, f32[1024,32]{1,0:T(8,128)S(1)}) custom-call(f32[1024,32]{1,0:T(8,128)S(1)} %reshape.16.right_ref, f32[1024,32]{1,0:T(8,128)S(1)} %reshape.17.guess_ref, bf16[16,64,384]{2,1,0:T(8,128)(2,1)S(1)} %copy-done, s32[1,2,4]{2,1,0:T(2,128)S(1)} %copy-done.1, s32[16,6]{1,0:T(8,128)S(1)} %copy.8.near_ref), custom_call_target="tpu_custom_call" | custom-call | tf_op jit(solution)/shard_map/pallas_call | solution.py:311
  102.2 0.9 reshape.18
  103.1 0.9 reshape.19
Async XLA Ops:
  0.6 3.0 %copy-start = (bf16[16,64,384]{2,1,0:T(8,128)(2,1)S(1)}, bf16[16,64,384]{2,1,0:T(8,128)(2,1)}, u32[]{:S(2)}) copy-start(bf16[16,64,384]{2,1,0:T(8,128)(2,1)} %couple_ref.1) | copy-start | bytes 2359300
  2.6 1.1 %copy-start.1 = (s32[1,2,4]{2,1,0:T(2,128)S(1)}, s32[1,2,4]{2,1,0:T(2,128)}, u32[]{:S(2)}) copy-start(s32[1,2,4]{2,1,0:T(2,128)} %lists_ref.1) | copy-start | bytes 100
